TPU v7x, 256 devices: a whole 4x4x8 slice. The times are simulated.
256 devices in a mesh: seq: 16 (over z, core), head: 4 (over x), dp: 4 (over y).
Axes of the slice: x: 4, y: 4, z: 8, core: 2. Of those that a mesh axis runs over, the one named last changes fastest.
Arguments:
- self_queries: bfloat16 [4, 2048, 2560], P('dp', ('seq', 'head')), may hold values from -8 to 8
- self_keys: bfloat16 [4, 2048, 2560], P('dp', ('seq', 'head')), may hold values from -4 to 4
- self_values: bfloat16 [4, 2048, 2560], P('dp', ('seq', 'head')), may hold values from -6 to 6
- self_cotangent: bfloat16 [4, 2048, 2560], P('dp', ('seq', 'head')), may hold values from -6 to 6
- text_queries: bfloat16 [4, 4096, 2560], P('dp', 'seq', 'head'), may hold values from -8 to 8
- memory_keys: bfloat16 [4, 2048, 2560], P('dp', 'seq', 'head'), may hold values from -4 to 4
- memory_values: bfloat16 [4, 2048, 2560], P('dp', 'seq', 'head'), may hold values from -6 to 6
- text_cotangent: bfloat16 [4, 4096, 2560], P('dp', 'seq', 'head'), may hold values from -6 to 6
- slopes: float32 [2, 20], P(None, 'head'), may hold values from 0.01 to 0.3
- page_counts: int32 [4, 4], P('dp'), may hold values from 1 to 1024, as said below
- page_cols: int32 [4, 4], P('dp'), may hold values from 4 to 64
- text_page: int32 [4, 4096], P('dp'), may hold values from 0 to 3, as said below
Outputs:
- self_query_grad: bfloat16 [4, 2048, 2560], P('dp', ('seq', 'head'))
- self_key_grad: bfloat16 [4, 2048, 2560], P('dp', ('seq', 'head'))
- self_value_grad: bfloat16 [4, 2048, 2560], P('dp', ('seq', 'head'))
- slope_grad: float32 [2, 20], P(None, 'head')
- text_query_grad: bfloat16 [4, 4096, 2560], P('dp', 'seq', 'head')
- memory_key_grad: bfloat16 [4, 2048, 2560], P('dp', 'seq', 'head')
- memory_value_grad: bfloat16 [4, 2048, 2560], P('dp', 'seq', 'head')
Inputs may be any that keep to these rules, and one draw needn't show every extreme that they name: `page_counts`: each pack's counts sum to 2048; one page of every pack has exactly 1024 patches. `text_page`: never falls along a pack's text rows; every page has at least one text row.
All inputs are finite; a program needn't handle non-finite values.
Results may differ from a plain program's by a relative error of at most 0.006.
Values may be sent and summed in bfloat16 or wider, within the bound.
No kernel may reach another device: no remote copies, remote signals or barrier semaphores. Data moves between devices by JAX's collectives and lax.ppermute only.
A program may use at most 128 MiB of HBM per device.

v0:
```python
import jax
import jax.numpy as jnp
from jax import lax
from jax.sharding import PartitionSpec as P

MASK_FILL = -1e30


def page_layout(counts, widths, patch_total):
    page_ends = jnp.cumsum(counts)
    starts = page_ends - counts
    positions = jnp.arange(patch_total, dtype=jnp.int32)
    page_ids = jnp.sum((positions[:, None] >= page_ends[None, :]).astype(jnp.int32), axis=1)
    one_hot = page_ids[:, None] == jnp.arange(counts.shape[0], dtype=jnp.int32)[None, :]
    page_start = jnp.sum(jnp.where(one_hot, starts[None, :], 0), axis=1)
    page_width = jnp.sum(jnp.where(one_hot, widths[None, :], 0), axis=1)
    offsets = positions - page_start
    return (page_ids, offsets // page_width, offsets % page_width)


def take_rows(vector, row_start, row_count):
    return lax.dynamic_slice_in_dim(vector, row_start, row_count, 0)


def heads_of(matrix, head_count):
    return matrix.reshape(matrix.shape[0], head_count, -1)


def alibi(slopes, query_layout, key_layout):
    row_gap = jnp.abs(query_layout[1][:, None] - key_layout[1][None, :]).astype(jnp.float32)
    col_gap = jnp.abs(query_layout[2][:, None] - key_layout[2][None, :]).astype(jnp.float32)
    same_page = query_layout[0][:, None] == key_layout[0][None, :]
    decay = -(slopes[0][:, None, None] * row_gap[None] + slopes[1][:, None, None] * col_gap[None])
    return (jnp.where(same_page[None], decay, MASK_FILL), row_gap, col_gap)


def query_side(queries, key_rows, value_rows, grad_rows, logit_bias):
    inv_root = queries.shape[2] ** (-0.5)
    scores = (
        jnp.einsum("rhs,khs->hrk", queries, key_rows, preferred_element_type=jnp.float32) * inv_root
        + logit_bias
    )
    row_max = jnp.max(scores, axis=2, keepdims=True)
    weights = jnp.exp(scores - row_max)
    row_total = jnp.sum(weights, axis=2, keepdims=True)
    softmax_w = weights / row_total
    log_total = (row_max + jnp.log(row_total))[:, :, 0]
    grad_probs = jnp.einsum(
        "rhs,khs->hrk", grad_rows, value_rows, preferred_element_type=jnp.float32
    )
    row_delta = jnp.sum(softmax_w * grad_probs, axis=2, keepdims=True)
    grad_scores = softmax_w * (grad_probs - row_delta)
    grad_scores_b = grad_scores.astype(jnp.bfloat16)
    query_grad = (
        jnp.einsum("hrk,khs->rhs", grad_scores_b, key_rows, preferred_element_type=jnp.float32)
        * inv_root
    )
    return (
        query_grad,
        grad_scores,
        grad_scores_b,
        softmax_w.astype(jnp.bfloat16),
        log_total,
        row_delta[:, :, 0],
    )


def key_terms(grad_scores_b, softmax_b, queries, grad_rows, row_count):
    inv_root = queries.shape[3] ** (-0.5)
    key_grad = (
        jnp.einsum("chrk,crhs->khs", grad_scores_b, queries, preferred_element_type=jnp.float32)
        * inv_root
    )
    value_grad = jnp.einsum(
        "chrk,crhs->khs", softmax_b, grad_rows, preferred_element_type=jnp.float32
    )
    return jnp.stack([key_grad.reshape(row_count, -1), value_grad.reshape(row_count, -1)], axis=1)


def local(
    self_queries,
    self_keys,
    self_values,
    self_cotangent,
    text_queries,
    memory_keys,
    memory_values,
    text_cotangent,
    slopes,
    page_counts,
    page_cols,
    text_page,
):
    head_count = slopes.shape[1]
    regrouped = (
        lax.all_to_all(self_queries[0], "head", split_axis=1, concat_axis=0, tiled=True),
        lax.all_to_all(self_keys[0], "head", split_axis=1, concat_axis=0, tiled=True),
        lax.all_to_all(self_values[0], "head", split_axis=1, concat_axis=0, tiled=True),
        lax.all_to_all(self_cotangent[0], "head", split_axis=1, concat_axis=0, tiled=True),
    )
    local_queries, local_keys, local_values, local_grads = regrouped
    patch_rows = local_queries.shape[0]
    all_keys, all_values = (
        lax.all_gather(local_keys, "seq", axis=0, tiled=True),
        lax.all_gather(local_values, "seq", axis=0, tiled=True),
    )
    patch_total = all_keys.shape[0]
    whole_layout = page_layout(page_counts[0], page_cols[0], patch_total)
    own_start = lax.axis_index("seq") * patch_rows
    own_layout = tuple((take_rows(item, own_start, patch_rows) for item in whole_layout))
    self_bias, row_gap, col_gap = alibi(slopes, own_layout, whole_layout)
    query_heads = heads_of(local_queries, head_count)
    grad_heads = heads_of(local_grads, head_count)
    self_dq, self_ds, self_ds_b, self_p_b, self_lse, self_delta = query_side(
        query_heads,
        heads_of(all_keys, head_count),
        heads_of(all_values, head_count),
        grad_heads,
        self_bias,
    )
    slope_local = -jnp.stack(
        [
            jnp.sum(self_ds * row_gap[None], axis=(1, 2)),
            jnp.sum(self_ds * col_gap[None], axis=(1, 2)),
        ]
    )
    self_ds_blocks = self_ds_b[None]
    self_p_blocks = self_p_b[None]
    query_blocks = query_heads[None]
    grad_blocks = grad_heads[None]
    self_pair = lax.psum_scatter(
        key_terms(
            self_ds_blocks,
            self_p_blocks,
            query_blocks,
            grad_blocks,
            patch_rows * lax.axis_size("seq"),
        ),
        "seq",
        scatter_dimension=0,
        tiled=True,
    )
    self_dk = self_pair[:, 0]
    self_dv = self_pair[:, 1]
    restored = (
        lax.all_to_all(
            self_dq.reshape(patch_rows, -1).astype(jnp.bfloat16),
            "head",
            split_axis=0,
            concat_axis=1,
            tiled=True,
        ),
        lax.all_to_all(
            self_dk.astype(jnp.bfloat16), "head", split_axis=0, concat_axis=1, tiled=True
        ),
        lax.all_to_all(
            self_dv.astype(jnp.bfloat16), "head", split_axis=0, concat_axis=1, tiled=True
        ),
    )
    slope_grad = lax.psum(slope_local, ("seq", "dp")) / patch_total
    memory_all_keys, memory_all_values = (
        lax.all_gather(memory_keys[0], "seq", axis=0, tiled=True),
        lax.all_gather(memory_values[0], "seq", axis=0, tiled=True),
    )
    memory_all_key_heads = heads_of(memory_all_keys, head_count)
    memory_all_value_heads = heads_of(memory_all_values, head_count)
    text_rows = text_queries.shape[1]
    text_start = lax.axis_index("seq") * text_rows
    text_ids = text_page[0]
    own_text = take_rows(text_ids, text_start, text_rows)
    text_query_heads = heads_of(text_queries[0], head_count)
    text_grad_heads = heads_of(text_cotangent[0], head_count)
    block_count = text_rows // text_rows
    text_query_blocks = text_query_heads.reshape(block_count, text_rows, head_count, -1)
    text_grad_blocks = text_grad_heads.reshape(block_count, text_rows, head_count, -1)

    def cross_block(inputs):
        block_queries, block_grads, block_pages = inputs
        block_bias = jnp.where(
            block_pages[:, None] == whole_layout[0][None, :], 0.0, MASK_FILL
        ).astype(jnp.float32)[None]
        result = query_side(
            block_queries, memory_all_key_heads, memory_all_value_heads, block_grads, block_bias
        )
        return (result[0], result[2], result[3], result[4], result[5])

    cross_out = lax.map(
        cross_block, (text_query_blocks, text_grad_blocks, own_text.reshape(block_count, text_rows))
    )
    text_dq = cross_out[0].reshape(text_rows, -1)
    text_ds_b = cross_out[1]
    text_p_b = cross_out[2]
    memory_pair = lax.psum_scatter(
        key_terms(
            text_ds_b,
            text_p_b,
            text_query_blocks,
            text_grad_blocks,
            patch_rows * lax.axis_size("seq"),
        ),
        "seq",
        scatter_dimension=0,
        tiled=True,
    )
    memory_dk = memory_pair[:, 0]
    memory_dv = memory_pair[:, 1]
    return (
        restored[0][None],
        restored[1][None],
        restored[2][None],
        slope_grad,
        text_dq.astype(jnp.bfloat16)[None],
        memory_dk.astype(jnp.bfloat16)[None],
        memory_dv.astype(jnp.bfloat16)[None],
    )


def solution(mesh):
    in_specs = (
        P("dp", ("seq", "head"), None),
        P("dp", ("seq", "head"), None),
        P("dp", ("seq", "head"), None),
        P("dp", ("seq", "head"), None),
        P("dp", "seq", "head"),
        P("dp", "seq", "head"),
        P("dp", "seq", "head"),
        P("dp", "seq", "head"),
        P(None, "head"),
        P("dp", None),
        P("dp", None),
        P("dp", None),
    )
    out_specs = (
        P("dp", ("seq", "head"), None),
        P("dp", ("seq", "head"), None),
        P("dp", ("seq", "head"), None),
        P(None, "head"),
        P("dp", "seq", "head"),
        P("dp", "seq", "head"),
        P("dp", "seq", "head"),
    )
    return jax.shard_map(local, mesh=mesh, in_specs=in_specs, out_specs=out_specs, check_vma=False)
```

profile of v0, /device:TPU:2, one launch (start us, length us, event | category | flops | bytes accessed | tf_op | source)
XLA Modules:
  0.0 406.0 jit_solution(9305916653580052399)
XLA Ops:
  8.3 10.0 %all_to_all.109 = bf16[32,4,640]{2,0,1:T(8,128)(2,1)} all-to-all(bf16[32,4,640]{2,0,1:T(8,128)(2,1)S(1)} %copy.117), channel_id=1, replica_groups=mesh['seq'=16,'head'=4,'dp'=4] {'head'}, dimensions={1} | all-to-all | bytes 327680 | tf_op jit(solution)/shard_map/all_to_all | solution.py:97
  19.4 9.2 %all_to_all.110 = bf16[32,4,640]{2,0,1:T(8,128)(2,1)} all-to-all(bf16[32,4,640]{2,0,1:T(8,128)(2,1)S(1)} %copy.122), channel_id=1, replica_groups=mesh['seq'=16,'head'=4,'dp'=4] {'head'}, dimensions={1} | all-to-all | bytes 327680 | tf_op jit(solution)/shard_map/all_to_all | solution.py:98
  32.1 4.7 %all-to-all-start = ((bf16[32,4,640]{2,0,1:T(8,128)(2,1)}), bf16[32,4,640]{2,0,1:T(8,128)(2,1)S(1)}, u32[]{:S(2)}, u32[]{:S(2)}) async-start(bf16[32,4,640]{2,0,1:T(8,128)(2,1)} %copy.116), calls=%async_computation | async-start | bytes 327680 | tf_op jit(solution)/shard_map/all_to_all | solution.py:96
  44.2 4.8 %all-to-all-start.2 = ((bf16[32,4,640]{2,0,1:T(8,128)(2,1)}), bf16[32,4,640]{2,0,1:T(8,128)(2,1)S(1)}, u32[]{:S(2)}, u32[]{:S(2)}) async-start(bf16[32,4,640]{2,0,1:T(8,128)(2,1)} %copy.121), calls=%async_computation.2 | async-start | bytes 327680 | tf_op jit(solution)/shard_map/all_to_all | solution.py:99
  49.4 4.3 %all-to-all-done.2 = bf16[32,4,640]{2,0,1:T(8,128)(2,1)S(1)} async-done(((bf16[32,4,640]{2,0,1:T(8,128)(2,1)}), bf16[32,4,640]{2,0,1:T(8,128)(2,1)S(1)}, u32[]{:S(2)}, u32[]{:S(2)}) %all-to-all-start.2) | async-done | bytes 163872 | tf_op jit(solution)/shard_map/all_to_all | solution.py:99
  54.1 6.2 %all-gather.7.cloned.1.call-done = bf16[2048,640]{1,0:T(8,128)(2,1)} async-done(((bf16[128,640]{1,0:T(8,128)(2,1)}), bf16[2048,640]{1,0:T(8,128)(2,1)}) %all-gather.7.cloned.1.call-update) | async-done | bytes 2621456 | tf_op jit(solution)/shard_map/all_gather | solution.py:104
  63.3 37.8 %all-gather.9.cloned.1.call-done = bf16[2048,640]{1,0:T(8,128)(2,1)} async-done(((bf16[128,640]{1,0:T(8,128)(2,1)}), bf16[2048,640]{1,0:T(8,128)(2,1)}) %all-gather.9.cloned.1.call-update) | async-done | bytes 2621456 | tf_op jit(solution)/shard_map/all_gather | solution.py:105
  101.0 4.5 %copy.123 = bf16[2048,640]{0,1:T(8,128)(2,1)} copy(bf16[2048,640]{1,0:T(8,128)(2,1)} %all-gather.9.cloned.1.call-done) | data formatting | bytes 5242880 | tf_op jit(solution)/shard_map/all_gather | solution.py:105
  119.8 6.0 %copy.131 = f32[2048,1,640]{2,0,1:T(8,128)} copy(f32[2048,1,640]{0,2,1:T(8,128)} %bitcast.79) | data formatting | bytes 10485760 | tf_op jit(solution)/shard_map/stack;reshape | solution.py:77
  125.8 8.0 %fusion.7 = f32[5,2048,128]{1,2,0:T(8,128)} fusion(bf16[128,5,128]{0,2,1:T(8,128)(2,1)S(1)} %copy.130, f32[5,128]{1,0:T(8,128)S(1)} %get-tuple-element.85, f32[5,128,2048]{2,1,0:T(8,128)} %copy-done.4), kind=kOutput, calls=%fused_computation.22 | convolution fusion | flops 339479168 | bytes 10652160 | tf_op jit(solution)/shard_map/chrk,crhs->khs/dot_general | solution.py:74
  133.7 5.9 %copy.132 = f32[2048,1,640]{2,0,1:T(8,128)} copy(f32[2048,1,640]{0,2,1:T(8,128)} %bitcast.84) | data formatting | bytes 10485760 | tf_op jit(solution)/shard_map/stack;reshape | solution.py:77
  139.6 8.8 %pad_maximum_fusion = f32[2048,2,640]{2,0,1:T(8,128)} fusion(f32[2048,1,640]{2,0,1:T(8,128)} %copy.132, f32[2048,1,640]{2,0,1:T(8,128)} %copy.131), kind=kLoop, calls=%fused_computation.2 | loop fusion | flops 2621440 | bytes 20971520 | tf_op jit(solution)/shard_map/stack | solution.py:77
  152.4 9.5 %fusion.29 = (f32[5,256]{1,0:T(8,128)S(1)}, f32[5,256,2048]{2,1,0:T(8,128)}) fusion(f32[256,2048]{1,0:T(8,128)} %compare_select_fusion, bf16[256,5,128]{0,2,1:T(8,128)(2,1)S(1)} %bitcast.87, bf16[2048,5,128]{0,2,1:T(8,128)(2,1)} %bitcast.104), kind=kOutput, calls=%fused_computation.62 | convolution fusion | flops 681576448 | bytes 15537152 | tf_op jit(solution)/shard_map/while/body/eval_jaxpr/sub | solution.py:44
  161.8 27.1 %all-gather.13.cloned.1.call-done = bf16[1,2048,640]{1,2,0:T(8,128)(2,1)} async-done(((bf16[1,128,640]{1,2,0:T(8,128)(2,1)}), bf16[1,2048,640]{1,2,0:T(8,128)(2,1)}) %all-gather.13.cloned.1.call-update) | async-done | bytes 2621456 | tf_op jit(solution)/shard_map/all_gather | solution.py:163
  189.0 6.1 %multiply_reduce_fusion = (f32[5,256]{1,0:T(8,128)S(1)}, f32[5,256,2048]{2,1,0:T(8,128)S(1)}) fusion(f32[5,256,2048]{2,1,0:T(8,128)} %get-tuple-element.90, f32[5,256]{1,0:T(8,128)S(1)} %get-tuple-element.89, bf16[256,5,128]{0,2,1:T(8,128)(2,1)S(1)} %bitcast.96, bf16[2048,5,128]{0,2,1:T(8,128)(2,1)} %bitcast.106), kind=kOutput, calls=%fused_computation.5 | convolution fusion | flops 678951680 | bytes 23930880 | tf_op jit(solution)/shard_map/while/body/eval_jaxpr/rhs,khs->hrk/dot_general | solution.py:48
  202.6 5.9 %copy.143 = f32[2048,1,640]{2,0,1:T(8,128)} copy(f32[2048,1,640]{0,2,1:T(8,128)} %bitcast.78) | data formatting | bytes 10485760 | tf_op jit(solution)/shard_map/stack;reshape | solution.py:77
  208.5 7.4 %fusion.3 = f32[5,2048,128]{1,2,0:T(8,128)} fusion(bf16[256,5,128]{0,2,1:T(8,128)(2,1)S(1)} %bitcast.97, f32[5,256,2048]{2,1,0:T(8,128)} %get-tuple-element.90, f32[5,256]{1,0:T(8,128)S(1)} %get-tuple-element.89), kind=kOutput, calls=%fused_computation.9 | convolution fusion | flops 676331520 | bytes 16061440 | tf_op jit(solution)/shard_map/chrk,crhs->khs/dot_general | solution.py:74
  215.9 5.9 %copy.144 = f32[2048,1,640]{2,0,1:T(8,128)} copy(f32[2048,1,640]{0,2,1:T(8,128)} %bitcast.85) | data formatting | bytes 10485760 | tf_op jit(solution)/shard_map/stack;reshape | solution.py:77
  221.9 8.7 %pad_maximum_fusion.1 = f32[2048,2,640]{2,0,1:T(8,128)} fusion(f32[2048,1,640]{2,0,1:T(8,128)} %copy.144, f32[2048,1,640]{2,0,1:T(8,128)} %copy.143), kind=kLoop, calls=%fused_computation.3 | loop fusion | flops 2621440 | bytes 20971520 | tf_op jit(solution)/shard_map/stack | solution.py:77
  230.6 5.3 %fusion.14 = bf16[5,256,128]{1,2,0:T(8,128)(2,1)S(1)} fusion(bf16[5,256,2048]{2,1,0:T(8,128)(2,1)} %copy-done.2, bf16[2048,5,128]{0,2,1:T(8,128)(2,1)} %bitcast.105), kind=kOutput, calls=%fused_computation.31 | convolution fusion | flops 671416320 | bytes 8192000 | tf_op jit(solution)/shard_map/while/body/eval_jaxpr/hrk,khs->rhs/dot_general | solution.py:55
  236.9 129.5 %psum.7 = f32[2,5]{1,0:T(2,128)S(1)} all-reduce(f32[2,5]{1,0:T(2,128)S(1)} %maximum_negate_fusion), channel_id=1, replica_groups=mesh['seq'=16,'head'=4,'dp'=4] {'seq','dp'}, use_global_device_ids=true, to_apply=%region_10.11 | all-reduce | flops 10 | bytes 80 | tf_op jit(solution)/shard_map/psum | solution.py:160
  369.9 4.8 %all-to-all-start.4 = ((bf16[4,32,640]{2,1,0:T(8,128)(2,1)}), bf16[4,32,640]{2,1,0:T(8,128)(2,1)S(1)}, u32[]{:S(2)}, u32[]{:S(2)}) async-start(bf16[4,32,640]{2,1,0:T(8,128)(2,1)} %convert_element_type.95), calls=%async_computation.4 | async-start | bytes 327680 | tf_op jit(solution)/shard_map/all_to_all | solution.py:146
  379.4 4.8 %all-to-all-start.5 = ((bf16[4,32,640]{2,1,0:T(8,128)(2,1)}), bf16[4,32,640]{2,1,0:T(8,128)(2,1)S(1)}, u32[]{:S(2)}, u32[]{:S(2)}) async-start(bf16[4,32,640]{2,1,0:T(8,128)(2,1)} %bitcast.21), calls=%async_computation.6 | async-start | bytes 327680 | tf_op jit(solution)/shard_map/all_to_all | solution.py:153
  388.9 4.8 %all-to-all-start.6 = ((bf16[4,32,640]{2,1,0:T(8,128)(2,1)}), bf16[4,32,640]{2,1,0:T(8,128)(2,1)S(1)}, u32[]{:S(2)}, u32[]{:S(2)}) async-start(bf16[4,32,640]{2,1,0:T(8,128)(2,1)} %bitcast.23), calls=%async_computation.7 | async-start | bytes 327680 | tf_op jit(solution)/shard_map/all_to_all | solution.py:156
  (101 shorter events, 61.8 us)
Async XLA Ops:
  7.2 143.6 %copy-start = (s32[1,4096]{1,0:T(1,128)S(1)}, s32[1,4096]{1,0:T(1,128)}, u32[]{:S(2)}) copy-start(s32[1,4096]{1,0:T(1,128)} %param.23) | copy-start | bytes 49156
  7.2 36.3 %copy-start.9 = (bf16[1,32,2560]{2,1,0:T(8,128)(2,1)S(1)}, bf16[1,32,2560]{2,1,0:T(8,128)(2,1)}, u32[]{:S(2)}) copy-start(bf16[1,32,2560]{2,1,0:T(8,128)(2,1)} %param.15) | copy-start | bytes 491524
  7.2 41.8 %copy-start.10 = (f32[2,5]{1,0:T(2,128)S(1)}, f32[2,5]{1,0:T(2,128)}, u32[]{:S(2)}) copy-start(f32[2,5]{1,0:T(2,128)} %param.20) | copy-start | bytes 124
  7.2 53.1 %all-gather.7.cloned.1.call-start = ((), (), s32[]{:S(2)}) async-start(), calls=%async_computation.9 | async-start | bytes 2785280 | tf_op jit(solution)/shard_map/all_gather | solution.py:104
  18.3 82.7 %all-gather.9.cloned.1.call-start = ((), (), s32[]{:S(2)}) async-start(), calls=%async_computation.10 | async-start | bytes 2785280 | tf_op jit(solution)/shard_map/all_gather | solution.py:105
  28.6 123.8 %all-gather.11.cloned.1.call-start = ((), (), s32[]{:S(2)}) async-start(), calls=%async_computation.13 | async-start | bytes 2785280 | tf_op jit(solution)/shard_map/all_gather | solution.py:162
  32.1 12.1 %all-to-all-start = ((bf16[32,4,640]{2,0,1:T(8,128)(2,1)}), bf16[32,4,640]{2,0,1:T(8,128)(2,1)S(1)}, u32[]{:S(2)}, u32[]{:S(2)}) async-start(bf16[32,4,640]{2,0,1:T(8,128)(2,1)} %copy.116), calls=%async_computation | async-start | bytes 327680 | tf_op jit(solution)/shard_map/all_to_all | solution.py:96
  36.8 152.2 %all-gather.13.cloned.1.call-start = ((), (), s32[]{:S(2)}) async-start(), calls=%async_computation.14 | async-start | bytes 2785280 | tf_op jit(solution)/shard_map/all_gather | solution.py:163
  44.2 9.5 %all-to-all-start.2 = ((bf16[32,4,640]{2,0,1:T(8,128)(2,1)}), bf16[32,4,640]{2,0,1:T(8,128)(2,1)S(1)}, u32[]{:S(2)}, u32[]{:S(2)}) async-start(bf16[32,4,640]{2,0,1:T(8,128)(2,1)} %copy.121), calls=%async_computation.2 | async-start | bytes 327680 | tf_op jit(solution)/shard_map/all_to_all | solution.py:99
  49.0 325.7 %reduce-scatter.3.cloned.1.call-start = ((), (), s32[]{:S(2)}) async-start(), calls=%async_computation.11 | async-start | bytes 11141120 | tf_op jit(solution)/shard_map/reduce_scatter | solution.py:131
  63.3 45.8 %copy-start.3 = (bf16[2048,640]{0,1:T(8,128)(2,1)}, bf16[2048,640]{0,1:T(8,128)(2,1)S(1)}, u32[]{:S(2)}) copy-start(bf16[2048,640]{0,1:T(8,128)(2,1)S(1)} %copy.118) | copy-start | bytes 7864324
  109.1 2.7 copy-start.4
  109.1 3.6 copy-start.7
  112.7 1.3 copy-start.5
  112.7 1.6 copy-start.6
  148.5 237.1 %reduce-scatter.5.cloned.1.call-start = ((), (), s32[]{:S(2)}) async-start(), calls=%async_computation.12 | async-start | bytes 11141120 | tf_op jit(solution)/shard_map/reduce_scatter | solution.py:193
  189.0 6.1 %slice-start = ((s8[10485760]{0:T(1024)(128)(4,1)}), s8[4194304]{0:T(1024)(128)(4,1)S(1)}, s32[]{:S(2)}) async-start(s8[10485760]{0:T(1024)(128)(4,1)} %bitcast.80), calls=%async_computation.15 | async-start | bytes 8388608
  189.0 7.3 %slice-start.1 = ((s8[10485760]{0:T(1024)(128)(4,1)}), s8[4194304]{0:T(1024)(128)(4,1)S(1)}, s32[]{:S(2)}) async-start(s8[10485760]{0:T(1024)(128)(4,1)} %bitcast.80), calls=%async_computation.16 | async-start | bytes 8388608
  189.0 7.9 %slice-start.2 = ((s8[10485760]{0:T(1024)(128)(4,1)}), s8[2097152]{0:T(1024)(128)(4,1)S(1)}, s32[]{:S(2)}) async-start(s8[10485760]{0:T(1024)(128)(4,1)} %bitcast.80), calls=%async_computation.17 | async-start | bytes 4194304
  198.6 4.0 copy-start.2
  236.9 162.3 %copy-start.1 = (s32[1,4096]{1,0:T(1,128)S(1)}, s32[1,4096]{1,0:T(1,128)}, u32[]{:S(2)}) copy-start(s32[1,4096]{1,0:T(1,128)} %param.23) | copy-start | bytes 49156
  369.9 9.5 %all-to-all-start.4 = ((bf16[4,32,640]{2,1,0:T(8,128)(2,1)}), bf16[4,32,640]{2,1,0:T(8,128)(2,1)S(1)}, u32[]{:S(2)}, u32[]{:S(2)}) async-start(bf16[4,32,640]{2,1,0:T(8,128)(2,1)} %convert_element_type.95), calls=%async_computation.4 | async-start | bytes 327680 | tf_op jit(solution)/shard_map/all_to_all | solution.py:146
  379.4 9.5 %all-to-all-start.5 = ((bf16[4,32,640]{2,1,0:T(8,128)(2,1)}), bf16[4,32,640]{2,1,0:T(8,128)(2,1)S(1)}, u32[]{:S(2)}, u32[]{:S(2)}) async-start(bf16[4,32,640]{2,1,0:T(8,128)(2,1)} %bitcast.21), calls=%async_computation.6 | async-start | bytes 327680 | tf_op jit(solution)/shard_map/all_to_all | solution.py:153
  388.9 9.5 %all-to-all-start.6 = ((bf16[4,32,640]{2,1,0:T(8,128)(2,1)}), bf16[4,32,640]{2,1,0:T(8,128)(2,1)S(1)}, u32[]{:S(2)}, u32[]{:S(2)}) async-start(bf16[4,32,640]{2,1,0:T(8,128)(2,1)} %bitcast.23), calls=%async_computation.7 | async-start | bytes 327680 | tf_op jit(solution)/shard_map/all_to_all | solution.py:156
  (1 other events, 1.0 us)
Sparse Core Ops, SparseCore 0:
  18.5 41.7 all-gather.6
  62.1 38.8 all-gather.8
  103.4 41.4 all-gather.10
  147.0 41.9 all-gather.12
  191.4 73.8 reduce-scatter.2
  267.7 74.0 reduce-scatter.4
where the time goes:
time: 408 us; the launch traced here: 406 us
  blocking collectives  149 us (37%)
  waiting for transfers between devices  83.5 us (20%)
  local copies, waits for them, and re-layouts  52.1 us (13%)
  matrix products  50.7 us (12%)
  other arithmetic  32.3 us (8%)
  starting transfers between devices  24.2 us (6%)
  between operations  14.4 us (4%)
    psum x1, blocking collectives, local(): slope_grad = lax.psum(slope_local, ('seq', 'dp')) / patch_total  129 us
    all_gather x1, waiting for transfers between devices, local(): lax.all_gather(local_values, 'seq', axis=0, tiled=True)  37.8 us
    all_gather x1, waiting for transfers between devices, local(): lax.all_gather(memory_values[0], 'seq', axis=0, tiled=True)  27.1 us
    another operation x4, local copies, waits for them, and re-layouts, key_terms(): jnp.stack([key_grad.reshape(row_count, -1), value_grad.reshape(row_count,...  23.7 us
    another operation x2, other arithmetic, key_terms(): jnp.stack([key_grad.reshape(row_count, -1), value_grad.reshape(row_count,...  17.5 us
    dot_general x2, matrix products, key_terms(): jnp.einsum('chrk,crhs->khs', softmax_b, grad_rows, preferred_element_type...  15.4 us
    unnamed x33, local copies, waits for them, and re-layouts  10.6 us
    all_to_all x1, blocking collectives, local(): lax.all_to_all(self_keys[0], 'head', split_axis=1, concat_axis=0, tiled=T...  10 us
  transfers between devices with their start and end apart: 11, of which 7 were waited for; matrix products, arithmetic and copies ran while one was open for 31% of the time, Pallas kernels for 0%

commit v1 on v0

--- a/solution.py
+++ b/solution.py
@@ -160,7 +160,12 @@
     slope_grad = lax.psum(slope_local, ("seq", "dp")) / patch_total
     memory_all_keys, memory_all_values = (
         lax.all_gather(memory_keys[0], "seq", axis=0, tiled=True),
-        lax.all_gather(memory_values[0], "seq", axis=0, tiled=True),
+        jnp.concatenate(
+            lax.all_to_all(
+                jnp.stack(lax.axis_size("seq") * [memory_values[0]], axis=0), "seq", 0, 0
+            ),
+            0,
+        ),
     )
     memory_all_key_heads = heads_of(memory_all_keys, head_count)
     memory_all_value_heads = heads_of(memory_all_values, head_count)

time: 408 us -> 466 us (1.14)
  waiting for transfers between devices: 83.5 us -> 127 us
  local copies, waits for them, and re-layouts: 52.1 us -> 63 us
    all_to_all x0 -> x1, waiting for transfers between devices: none -> 69.1 us  [local(): lax.all_to_all(jnp.stack(lax.axis_size('seq') * [memory_values[0]], axis=...]
    all_gather x1 -> x0, waiting for transfers between devices: 27.1 us -> none  [local(): lax.all_gather(memory_values[0], 'seq', axis=0, tiled=True)]
    another operation x0 -> x3, local copies, waits for them, and re-layouts: none -> 7.37 us  [the longest x1 5.23 us: heads_of(): return matrix.reshape(matrix.shape[0], head_count, -1)]
    all_to_all x0 -> x1, local copies, waits for them, and re-layouts: none -> 4.93 us  [local(): lax.all_to_all(jnp.stack(lax.axis_size('seq') * [memory_values[0]], axis=...]
    unnamed x33 -> x34, local copies, waits for them, and re-layouts: 10.6 us -> 9.19 us
  transfers between devices with their start and end apart: 11 -> 11, of which waited for: 7 -> 7; matrix products, arithmetic and copies ran while one was open for 31% -> 30% of each run, Pallas kernels for 0% -> 0%
where the time goes in v1:
time: 466 us; the launch traced here: 464 us
  blocking collectives  148 us (32%)
  waiting for transfers between devices  127 us (27%)
  local copies, waits for them, and re-layouts  63 us (14%)
  matrix products  50.8 us (11%)
  other arithmetic  32.2 us (7%)
  starting transfers between devices  28.7 us (6%)
  between operations  14.1 us (3%)
    psum x1, blocking collectives, local(): slope_grad = lax.psum(slope_local, ('seq', 'dp')) / patch_total  129 us
    all_to_all x1, waiting for transfers between devices, local(): lax.all_to_all(jnp.stack(lax.axis_size('seq') * [memory_values[0]], axis=...  69.1 us
    all_gather x1, waiting for transfers between devices, local(): lax.all_gather(local_values, 'seq', axis=0, tiled=True)  37.8 us
    another operation x4, local copies, waits for them, and re-layouts, key_terms(): jnp.stack([key_grad.reshape(row_count, -1), value_grad.reshape(row_count,...  23.7 us
    another operation x2, other arithmetic, key_terms(): jnp.stack([key_grad.reshape(row_count, -1), value_grad.reshape(row_count,...  17.4 us
    dot_general x2, matrix products, key_terms(): jnp.einsum('chrk,crhs->khs', softmax_b, grad_rows, preferred_element_type...  15.3 us
    all_to_all x1, blocking collectives, local(): lax.all_to_all(self_keys[0], 'head', split_axis=1, concat_axis=0, tiled=T...  10 us
    sub x1, matrix products, query_side(): weights = jnp.exp(scores - row_max)  9.55 us
  transfers between devices with their start and end apart: 11, of which 7 were waited for; matrix products, arithmetic and copies ran while one was open for 30% of the time, Pallas kernels for 0%

profile of v1, /device:TPU:2, one launch (start us, length us, event | category | flops | bytes accessed | tf_op | source)
XLA Modules:
  0.0 463.9 jit_solution(15283107263724420395)
XLA Ops:
  8.3 10.0 %all_to_all.114 = bf16[32,4,640]{2,0,1:T(8,128)(2,1)} all-to-all(bf16[32,4,640]{2,0,1:T(8,128)(2,1)S(1)} %copy.118), channel_id=1, replica_groups=mesh['seq'=16,'head'=4,'dp'=4] {'head'}, dimensions={1} | all-to-all | bytes 327680 | tf_op jit(solution)/shard_map/all_to_all | solution.py:97
  19.4 9.2 %all_to_all.115 = bf16[32,4,640]{2,0,1:T(8,128)(2,1)} all-to-all(bf16[32,4,640]{2,0,1:T(8,128)(2,1)S(1)} %copy.123), channel_id=1, replica_groups=mesh['seq'=16,'head'=4,'dp'=4] {'head'}, dimensions={1} | all-to-all | bytes 327680 | tf_op jit(solution)/shard_map/all_to_all | solution.py:98
  30.3 4.8 %all-to-all-start = ((bf16[32,4,640]{2,0,1:T(8,128)(2,1)}), bf16[32,4,640]{2,0,1:T(8,128)(2,1)S(1)}, u32[]{:S(2)}, u32[]{:S(2)}) async-start(bf16[32,4,640]{2,0,1:T(8,128)(2,1)} %copy.117), calls=%async_computation | async-start | bytes 327680 | tf_op jit(solution)/shard_map/all_to_all | solution.py:96
  42.4 4.8 %all-to-all-start.2 = ((bf16[32,4,640]{2,0,1:T(8,128)(2,1)}), bf16[32,4,640]{2,0,1:T(8,128)(2,1)S(1)}, u32[]{:S(2)}, u32[]{:S(2)}) async-start(bf16[32,4,640]{2,0,1:T(8,128)(2,1)} %copy.122), calls=%async_computation.2 | async-start | bytes 327680 | tf_op jit(solution)/shard_map/all_to_all | solution.py:99
  52.3 7.9 %all-gather.5.cloned.1.call-done = bf16[2048,640]{1,0:T(8,128)(2,1)} async-done(((bf16[128,640]{1,0:T(8,128)(2,1)}), bf16[2048,640]{1,0:T(8,128)(2,1)}) %all-gather.5.cloned.1.call-update) | async-done | bytes 2621456 | tf_op jit(solution)/shard_map/all_gather | solution.py:104
  63.3 37.8 %all-gather.7.cloned.1.call-done = bf16[2048,640]{1,0:T(8,128)(2,1)} async-done(((bf16[128,640]{1,0:T(8,128)(2,1)}), bf16[2048,640]{1,0:T(8,128)(2,1)}) %all-gather.7.cloned.1.call-update) | async-done | bytes 2621456 | tf_op jit(solution)/shard_map/all_gather | solution.py:105
  119.8 6.0 %copy.132 = f32[2048,1,640]{2,0,1:T(8,128)} copy(f32[2048,1,640]{0,2,1:T(8,128)} %bitcast.81) | data formatting | bytes 10485760 | tf_op jit(solution)/shard_map/stack;reshape | solution.py:77
  125.8 8.0 %fusion.7 = f32[5,2048,128]{1,2,0:T(8,128)} fusion(bf16[128,5,128]{0,2,1:T(8,128)(2,1)S(1)} %copy.131, f32[5,128]{1,0:T(8,128)S(1)} %get-tuple-element.85, f32[5,128,2048]{2,1,0:T(8,128)} %copy-done.4), kind=kOutput, calls=%fused_computation.22 | convolution fusion | flops 339479168 | bytes 10652160 | tf_op jit(solution)/shard_map/chrk,crhs->khs/dot_general | solution.py:74
  133.7 5.9 %copy.133 = f32[2048,1,640]{2,0,1:T(8,128)} copy(f32[2048,1,640]{0,2,1:T(8,128)} %bitcast.86) | data formatting | bytes 10485760 | tf_op jit(solution)/shard_map/stack;reshape | solution.py:77
  139.6 8.8 %pad_maximum_fusion = f32[2048,2,640]{2,0,1:T(8,128)} fusion(f32[2048,1,640]{2,0,1:T(8,128)} %copy.133, f32[2048,1,640]{2,0,1:T(8,128)} %copy.132), kind=kLoop, calls=%fused_computation.2 | loop fusion | flops 2621440 | bytes 20971520 | tf_op jit(solution)/shard_map/stack | solution.py:77
  159.2 69.1 %all-to-all-done.7 = bf16[16,128,640]{1,2,0:T(8,128)(2,1)} async-done(((bf16[16,128,640]{1,2,0:T(8,128)(2,1)}), bf16[16,128,640]{1,2,0:T(8,128)(2,1)}, u32[]{:S(2)}, u32[]{:S(2)}) %all-to-all-start.7) | async-done | bytes 2621472 | tf_op jit(solution)/shard_map/all_to_all | solution.py:164
  228.3 4.9 %copy.142 = bf16[16,128,640]{1,0,2:T(8,128)(2,1)} copy(bf16[16,128,640]{1,2,0:T(8,128)(2,1)} %all-to-all-done.7) | data formatting | bytes 5242880 | tf_op jit(solution)/shard_map/all_to_all | solution.py:164
  233.2 5.2 %reshape_reshape.3 = bf16[2048,5,128]{0,2,1:T(8,128)(2,1)} reshape(bf16[16,128,640]{1,0,2:T(8,128)(2,1)} %copy.142) | data formatting | bytes 5242880 | tf_op jit(solution)/shard_map/reshape;reshape | solution.py:26
  238.4 9.5 %fusion.29 = (f32[5,256]{1,0:T(8,128)S(1)}, f32[5,256,2048]{2,1,0:T(8,128)}) fusion(f32[256,2048]{1,0:T(8,128)} %compare_select_fusion, bf16[256,5,128]{0,2,1:T(8,128)(2,1)S(1)} %bitcast.89, bf16[2048,5,128]{0,2,1:T(8,128)(2,1)} %bitcast.107), kind=kOutput, calls=%fused_computation.62 | convolution fusion | flops 681576448 | bytes 15537152 | tf_op jit(solution)/shard_map/while/body/eval_jaxpr/sub | solution.py:44
  248.0 6.3 %multiply_reduce_fusion = (f32[5,256]{1,0:T(8,128)S(1)}, f32[5,256,2048]{2,1,0:T(8,128)S(1)}) fusion(f32[5,256,2048]{2,1,0:T(8,128)} %get-tuple-element.90, f32[5,256]{1,0:T(8,128)S(1)} %get-tuple-element.89, bf16[256,5,128]{0,2,1:T(8,128)(2,1)S(1)} %bitcast.98, bf16[2048,5,128]{0,2,1:T(8,128)(2,1)} %reshape_reshape.3), kind=kOutput, calls=%fused_computation.5 | convolution fusion | flops 678951680 | bytes 23930880 | tf_op jit(solution)/shard_map/while/body/eval_jaxpr/rhs,khs->hrk/dot_general | solution.py:48
  262.0 5.9 %copy.145 = f32[2048,1,640]{2,0,1:T(8,128)} copy(f32[2048,1,640]{0,2,1:T(8,128)} %bitcast.80) | data formatting | bytes 10485760 | tf_op jit(solution)/shard_map/stack;reshape | solution.py:77
  268.0 7.4 %fusion.3 = f32[5,2048,128]{1,2,0:T(8,128)} fusion(bf16[256,5,128]{0,2,1:T(8,128)(2,1)S(1)} %bitcast.99, f32[5,256,2048]{2,1,0:T(8,128)} %get-tuple-element.90, f32[5,256]{1,0:T(8,128)S(1)} %get-tuple-element.89), kind=kOutput, calls=%fused_computation.9 | convolution fusion | flops 676331520 | bytes 16061440 | tf_op jit(solution)/shard_map/chrk,crhs->khs/dot_general | solution.py:74
  275.3 5.9 %copy.146 = f32[2048,1,640]{2,0,1:T(8,128)} copy(f32[2048,1,640]{0,2,1:T(8,128)} %bitcast.87) | data formatting | bytes 10485760 | tf_op jit(solution)/shard_map/stack;reshape | solution.py:77
  281.2 8.6 %pad_maximum_fusion.1 = f32[2048,2,640]{2,0,1:T(8,128)} fusion(f32[2048,1,640]{2,0,1:T(8,128)} %copy.146, f32[2048,1,640]{2,0,1:T(8,128)} %copy.145), kind=kLoop, calls=%fused_computation.3 | loop fusion | flops 2621440 | bytes 20971520 | tf_op jit(solution)/shard_map/stack | solution.py:77
  289.8 5.2 %fusion.14 = bf16[5,256,128]{1,2,0:T(8,128)(2,1)S(1)} fusion(bf16[5,256,2048]{2,1,0:T(8,128)(2,1)} %copy-done.2, bf16[2048,5,128]{0,2,1:T(8,128)(2,1)} %bitcast.108), kind=kOutput, calls=%fused_computation.31 | convolution fusion | flops 671416320 | bytes 8192000 | tf_op jit(solution)/shard_map/while/body/eval_jaxpr/hrk,khs->rhs/dot_general | solution.py:55
  295.9 128.6 %psum.7 = f32[2,5]{1,0:T(2,128)S(1)} all-reduce(f32[2,5]{1,0:T(2,128)S(1)} %maximum_negate_fusion), channel_id=1, replica_groups=mesh['seq'=16,'head'=4,'dp'=4] {'seq','dp'}, use_global_device_ids=true, to_apply=%region_10.11 | all-reduce | flops 10 | bytes 80 | tf_op jit(solution)/shard_map/psum | solution.py:160
  428.1 4.8 %all-to-all-start.4 = ((bf16[4,32,640]{2,1,0:T(8,128)(2,1)}), bf16[4,32,640]{2,1,0:T(8,128)(2,1)S(1)}, u32[]{:S(2)}, u32[]{:S(2)}) async-start(bf16[4,32,640]{2,1,0:T(8,128)(2,1)} %convert_element_type.95), calls=%async_computation.4 | async-start | bytes 327680 | tf_op jit(solution)/shard_map/all_to_all | solution.py:146
  437.6 4.8 %all-to-all-start.5 = ((bf16[4,32,640]{2,1,0:T(8,128)(2,1)}), bf16[4,32,640]{2,1,0:T(8,128)(2,1)S(1)}, u32[]{:S(2)}, u32[]{:S(2)}) async-start(bf16[4,32,640]{2,1,0:T(8,128)(2,1)} %bitcast.21), calls=%async_computation.6 | async-start | bytes 327680 | tf_op jit(solution)/shard_map/all_to_all | solution.py:153
  447.1 4.8 %all-to-all-start.6 = ((bf16[4,32,640]{2,1,0:T(8,128)(2,1)}), bf16[4,32,640]{2,1,0:T(8,128)(2,1)S(1)}, u32[]{:S(2)}, u32[]{:S(2)}) async-start(bf16[4,32,640]{2,1,0:T(8,128)(2,1)} %bitcast.23), calls=%async_computation.7 | async-start | bytes 327680 | tf_op jit(solution)/shard_map/all_to_all | solution.py:156
  (105 shorter events, 75.7 us)
Async XLA Ops:
  7.2 150.4 %copy-start = (s32[1,4096]{1,0:T(1,128)S(1)}, s32[1,4096]{1,0:T(1,128)}, u32[]{:S(2)}) copy-start(s32[1,4096]{1,0:T(1,128)} %param.23) | copy-start | bytes 49156
  7.2 34.5 %copy-start.9 = (bf16[1,32,2560]{2,1,0:T(8,128)(2,1)S(1)}, bf16[1,32,2560]{2,1,0:T(8,128)(2,1)}, u32[]{:S(2)}) copy-start(bf16[1,32,2560]{2,1,0:T(8,128)(2,1)} %param.15) | copy-start | bytes 491524
  7.2 40.0 %copy-start.11 = (f32[2,5]{1,0:T(2,128)S(1)}, f32[2,5]{1,0:T(2,128)}, u32[]{:S(2)}) copy-start(f32[2,5]{1,0:T(2,128)} %param.20) | copy-start | bytes 124
  7.2 53.1 %all-gather.5.cloned.1.call-start = ((), (), s32[]{:S(2)}) async-start(), calls=%async_computation.10 | async-start | bytes 2785280 | tf_op jit(solution)/shard_map/all_gather | solution.py:104
  18.3 82.7 %all-gather.7.cloned.1.call-start = ((), (), s32[]{:S(2)}) async-start(), calls=%async_computation.11 | async-start | bytes 2785280 | tf_op jit(solution)/shard_map/all_gather | solution.py:105
  30.3 12.1 %all-to-all-start = ((bf16[32,4,640]{2,0,1:T(8,128)(2,1)}), bf16[32,4,640]{2,0,1:T(8,128)(2,1)S(1)}, u32[]{:S(2)}, u32[]{:S(2)}) async-start(bf16[32,4,640]{2,0,1:T(8,128)(2,1)} %copy.117), calls=%async_computation | async-start | bytes 327680 | tf_op jit(solution)/shard_map/all_to_all | solution.py:96
  35.0 203.4 %all-gather.9.cloned.1.call-start = ((), (), s32[]{:S(2)}) async-start(), calls=%async_computation.14 | async-start | bytes 2785280 | tf_op jit(solution)/shard_map/all_gather | solution.py:162
  42.4 9.5 %all-to-all-start.2 = ((bf16[32,4,640]{2,0,1:T(8,128)(2,1)}), bf16[32,4,640]{2,0,1:T(8,128)(2,1)S(1)}, u32[]{:S(2)}, u32[]{:S(2)}) async-start(bf16[32,4,640]{2,0,1:T(8,128)(2,1)} %copy.122), calls=%async_computation.2 | async-start | bytes 327680 | tf_op jit(solution)/shard_map/all_to_all | solution.py:99
  47.2 385.7 %reduce-scatter.3.cloned.1.call-start = ((), (), s32[]{:S(2)}) async-start(), calls=%async_computation.12 | async-start | bytes 11141120 | tf_op jit(solution)/shard_map/reduce_scatter | solution.py:131
  63.3 45.8 %copy-start.3 = (bf16[2048,640]{0,1:T(8,128)(2,1)}, bf16[2048,640]{0,1:T(8,128)(2,1)S(1)}, u32[]{:S(2)}) copy-start(bf16[2048,640]{0,1:T(8,128)(2,1)S(1)} %copy.119) | copy-start | bytes 7864324
  109.1 2.7 copy-start.4
  109.1 3.6 copy-start.7
  112.7 1.6 copy-start.6
  148.5 7.7 %copy-start.8 = (bf16[1,256,640]{2,1,0:T(8,128)(2,1)S(1)}, bf16[1,256,640]{2,1,0:T(8,128)(2,1)}, u32[]{:S(2)}) copy-start(bf16[1,256,640]{2,1,0:T(8,128)(2,1)} %param.16) | copy-start | bytes 983044
  151.5 76.8 %all-to-all-start.7 = ((bf16[16,128,640]{1,2,0:T(8,128)(2,1)}), bf16[16,128,640]{1,2,0:T(8,128)(2,1)}, u32[]{:S(2)}, u32[]{:S(2)}) async-start(bf16[16,128,640]{1,2,0:T(8,128)(2,1)} %stack.22), calls=%async_computation.8 | async-start | bytes 5242880 | tf_op jit(solution)/shard_map/all_to_all | solution.py:164
  156.2 287.6 %reduce-scatter.5.cloned.1.call-start = ((), (), s32[]{:S(2)}) async-start(), calls=%async_computation.13 | async-start | bytes 11141120 | tf_op jit(solution)/shard_map/reduce_scatter | solution.py:198
  248.0 6.3 %slice-start = ((s8[10485760]{0:T(1024)(128)(4,1)}), s8[4194304]{0:T(1024)(128)(4,1)S(1)}, s32[]{:S(2)}) async-start(s8[10485760]{0:T(1024)(128)(4,1)} %bitcast.82), calls=%async_computation.15 | async-start | bytes 8388608
  248.0 7.6 %slice-start.1 = ((s8[10485760]{0:T(1024)(128)(4,1)}), s8[4194304]{0:T(1024)(128)(4,1)S(1)}, s32[]{:S(2)}) async-start(s8[10485760]{0:T(1024)(128)(4,1)} %bitcast.82), calls=%async_computation.16 | async-start | bytes 8388608
  248.0 8.3 %slice-start.2 = ((s8[10485760]{0:T(1024)(128)(4,1)}), s8[2097152]{0:T(1024)(128)(4,1)S(1)}, s32[]{:S(2)}) async-start(s8[10485760]{0:T(1024)(128)(4,1)} %bitcast.82), calls=%async_computation.17 | async-start | bytes 4194304
  258.0 4.0 copy-start.2
  295.9 161.5 %copy-start.1 = (s32[1,4096]{1,0:T(1,128)S(1)}, s32[1,4096]{1,0:T(1,128)}, u32[]{:S(2)}) copy-start(s32[1,4096]{1,0:T(1,128)} %param.23) | copy-start | bytes 49156
  428.1 9.5 %all-to-all-start.4 = ((bf16[4,32,640]{2,1,0:T(8,128)(2,1)}), bf16[4,32,640]{2,1,0:T(8,128)(2,1)S(1)}, u32[]{:S(2)}, u32[]{:S(2)}) async-start(bf16[4,32,640]{2,1,0:T(8,128)(2,1)} %convert_element_type.95), calls=%async_computation.4 | async-start | bytes 327680 | tf_op jit(solution)/shard_map/all_to_all | solution.py:146
  437.6 9.5 %all-to-all-start.5 = ((bf16[4,32,640]{2,1,0:T(8,128)(2,1)}), bf16[4,32,640]{2,1,0:T(8,128)(2,1)S(1)}, u32[]{:S(2)}, u32[]{:S(2)}) async-start(bf16[4,32,640]{2,1,0:T(8,128)(2,1)} %bitcast.21), calls=%async_computation.6 | async-start | bytes 327680 | tf_op jit(solution)/shard_map/all_to_all | solution.py:153
  447.1 9.5 %all-to-all-start.6 = ((bf16[4,32,640]{2,1,0:T(8,128)(2,1)}), bf16[4,32,640]{2,1,0:T(8,128)(2,1)S(1)}, u32[]{:S(2)}, u32[]{:S(2)}) async-start(bf16[4,32,640]{2,1,0:T(8,128)(2,1)} %bitcast.23), calls=%async_computation.7 | async-start | bytes 327680 | tf_op jit(solution)/shard_map/all_to_all | solution.py:156
  (2 other events, 2.2 us)
Sparse Core Ops, SparseCore 0:
  18.5 41.7 all-gather.4
  62.1 38.8 all-gather.6
  103.4 41.4 all-gather.8
  148.6 126.5 reduce-scatter.2
  289.9 75.9 reduce-scatter.4
